TPU v7x, 512 devices: a whole 4x4x16 slice. The times are simulated.
512 devices in a mesh: group: 4 (over z_hi), dp: 32 (over y, z_lo, core), tensor: 4 (over x).
Axes of the slice: x: 4, y: 4, z: 16 (z_hi: 4, z_lo: 4; z = z_hi * 4 + z_lo), core: 2. Of those that a mesh axis runs over, the one named last changes fastest.
Arguments:
- queries: bfloat16 [16384, 4096], P(('group', 'dp'), 'tensor'), may hold values from -16 to 16
- span_state: bfloat16 [16384, 4096], P(('group', 'dp'), 'tensor'), may hold values from -6 to 6
- neigh_state: bfloat16 [65536, 4096], P(('group', 'dp'), 'tensor'), may hold values from -24 to 24
- counts: int32 [4, 64], P('group'), may hold values from 1 to 2
- norm_gain: float32 [4096], P('tensor'), may hold values from 0.5 to 1.5
- head_gate: float32 [32], P('tensor'), may hold values from 0.3 to 1.5
- out_grad: bfloat16 [16384, 4096], P(('group', 'dp'), 'tensor'), may hold values from -6 to 6
Outputs:
- cross_output: bfloat16 [16384, 4096], P(('group', 'dp'), 'tensor')
- query_grad: bfloat16 [16384, 4096], P(('group', 'dp'), 'tensor')
- span_grad: bfloat16 [16384, 4096], P(('group', 'dp'), 'tensor')
- neighbour_grad: bfloat16 [65536, 4096], P(('group', 'dp'), 'tensor')
- gate_grad: float32 [32], P('tensor')
Inputs may be any that keep to these rules, and one draw needn't show every extreme that they name: Slot j of span c holds a retrieved neighbour exactly when j < counts[c].
All inputs are finite; a program needn't handle non-finite values.
Results may differ from a plain program's by a relative error of at most 0.0095.
The roundings to bfloat16 on the way count: a program that leaves them out, or rounds other values in their place, can miss the bound.
Values may be sent and summed in bfloat16 or wider, within the bound.
No kernel may reach another device: no remote copies, remote signals or barrier semaphores. Data moves between devices by JAX's collectives and lax.ppermute only.
A program may use at most 64 MiB of HBM per device.

v0:
```python
import math
import jax
import jax.numpy as jnp
from jax import lax
from jax.sharding import PartitionSpec as P

CH = 64
NB = 2
NL = 128
epsilon = 1e-05
masked_score = -1e30


def shifted(value, axis, steps):
    count = lax.axis_size(axis)
    leading, last = (max(0, -steps), min(count, count - steps))
    return lax.ppermute(value, axis, [(source, source + steps) for source in range(leading, last)])


def product(form, left, right):
    return jnp.einsum(form, left, right, preferred_element_type=jnp.float32)


def encoder_forward(normed, neighbours, contexts):
    slot_count = normed.shape[1]
    spread = jnp.broadcast_to(
        contexts[:, None], (contexts.shape[0], slot_count) + contexts.shape[1:]
    )
    all_keys = jnp.concatenate([normed, spread], axis=2)
    scores = product("cjqhd,cjkhd->cjhqk", normed, all_keys) / normed.shape[-1]
    powers = jnp.exp(scores)
    weights = powers / jnp.sum(powers, axis=-1, keepdims=True)
    rounded = weights.astype(jnp.bfloat16)
    mixture = product("cjhqk,cjkhd->cjqhd", rounded, all_keys)
    encoded = (neighbours.astype(jnp.float32) + mixture).astype(jnp.bfloat16)
    return (encoded, (all_keys, weights, rounded, mixture))


def encoder_backward(grad_encoded, normed, saved):
    all_keys, weights, rounded, mixture = saved
    grad_rounded = grad_encoded.astype(jnp.bfloat16)
    grad_weights = product("cjqhd,cjkhd->cjhqk", grad_rounded, all_keys)
    offset = jnp.moveaxis(jnp.sum(grad_encoded * mixture, axis=-1), -1, 2)[..., None]
    score_grad = (weights * (grad_weights - offset) / normed.shape[-1]).astype(jnp.bfloat16)
    normed_grad = product("cjhqk,cjkhd->cjqhd", score_grad, all_keys)
    key_grad = product("cjhqk,cjqhd->cjkhd", score_grad, normed) + product(
        "cjhqk,cjqhd->cjkhd", rounded, grad_rounded
    )
    length = normed.shape[2]
    normed_grad = normed_grad + key_grad[:, :, :length]
    context_grad = jnp.sum(key_grad[:, :, length:], axis=1)
    return (normed_grad, context_grad)


def cross_attend(blocks, grad_blocks, keys, usable, present, gate_tanh):
    scale = 1.0 / math.sqrt(blocks.shape[-1])
    scores = product("brhd,bmhd->bhrm", blocks, keys) * scale
    scores = jnp.where(usable[:, None, None, :], scores, masked_score)
    highest = jnp.max(scores, axis=-1, keepdims=True)
    powers = jnp.exp(scores - highest)
    weights = powers / jnp.sum(powers, axis=-1, keepdims=True)
    rounded = weights.astype(jnp.bfloat16)
    attended = product("bhrm,bmhd->brhd", rounded, keys)
    present_mask = present[:, None, None, None]
    attended = jnp.where(present_mask, attended, 0.0)
    output = (gate_tanh[:, None] * attended).astype(jnp.bfloat16)
    grad_output = grad_blocks.astype(jnp.float32)
    gate_term = jnp.sum(grad_output * attended, axis=(0, 1, 3))
    att_grad = jnp.where(present_mask, gate_tanh[:, None] * grad_output, 0.0)
    grad_rounded = att_grad.astype(jnp.bfloat16)
    grad_weights = product("brhd,bmhd->bhrm", grad_rounded, keys)
    offset = jnp.moveaxis(jnp.sum(att_grad * attended, axis=-1), -1, 1)[..., None]
    score_grad = (weights * (grad_weights - offset) * scale).astype(jnp.bfloat16)
    query_grad = product("bhrm,bmhd->brhd", score_grad, keys).astype(jnp.bfloat16)
    key_grad = product("bhrm,brhd->bmhd", score_grad, blocks) + product(
        "bhrm,brhd->bmhd", rounded, grad_rounded
    )
    return (output, query_grad, key_grad, gate_term)


def shards(queries, span_state, neigh_state, counts, norm_gain, head_gate, out_grad):
    head_count = head_gate.shape[0]
    local_width = queries.shape[1]
    head_dim = local_width // head_count
    row_count = queries.shape[0]
    span_count = row_count // CH
    seq_spans = counts.shape[1]
    lead = CH - 1

    def blockify(matrix):
        return matrix.reshape(-1, CH, head_count, head_dim)

    neighbours = neigh_state.reshape(span_count, NB, NL, head_count, head_dim)
    contexts = span_state.reshape(span_count, CH, head_count, head_dim)
    gains = norm_gain.reshape(head_count, head_dim)
    floats = neighbours.astype(jnp.float32)
    square_sum = lax.psum(jnp.sum(floats * floats, axis=(3, 4)), "tensor")
    full_width = lax.axis_size("tensor") * local_width
    inverse = lax.rsqrt(square_sum / full_width + epsilon)[..., None, None]
    scaled = floats * inverse
    normed = (scaled * gains).astype(jnp.bfloat16)
    encoded, saved = encoder_forward(normed, neighbours, contexts)
    line_index = lax.axis_index("dp")
    first_span = line_index * span_count
    flat_counts = counts.reshape(-1)
    own_counts = lax.dynamic_slice_in_dim(flat_counts, first_span, span_count)
    gate_tanh = jnp.tanh(head_gate)
    usable = jnp.repeat(jnp.arange(NB)[None, :] < own_counts[:, None], NL, axis=1)
    present = own_counts > 0
    keys = encoded.reshape(span_count, NB * NL, head_count, head_dim)
    kept = row_count - lead
    padding = jnp.zeros((lead, local_width), jnp.bfloat16)
    blocks = blockify(jnp.concatenate([queries[lead:], padding], axis=0))
    grad_blocks = blockify(jnp.concatenate([out_grad[lead:], padding], axis=0))
    earlier_keys = shifted(keys[span_count - 1], "dp", 1)
    earlier_count = lax.dynamic_index_in_dim(
        flat_counts, jnp.maximum(first_span - 1, 0), keepdims=False
    )
    earlier_present = jnp.logical_and(first_span % seq_spans > 0, earlier_count > 0)
    earlier_usable = jnp.repeat(jnp.arange(NB) < earlier_count, NL)
    front_row = jnp.zeros((1, local_width), jnp.bfloat16)
    first_block = blockify(jnp.concatenate([front_row, queries[:lead]], axis=0))
    first_grad = blockify(jnp.concatenate([front_row, out_grad[:lead]], axis=0))
    front_out, front_query, front_keys, front_term = cross_attend(
        first_block,
        first_grad,
        earlier_keys[None],
        earlier_usable[None],
        earlier_present[None],
        gate_tanh,
    )
    local_out, local_query, key_grad, local_term = cross_attend(
        blocks, grad_blocks, keys, usable, present, gate_tanh
    )
    returned = shifted(front_keys[0].astype(jnp.bfloat16), "dp", -1).astype(jnp.float32)
    key_grad = key_grad.at[span_count - 1].add(returned)
    cross_output = jnp.concatenate(
        [front_out.reshape(CH, local_width)[1:], local_out.reshape(row_count, local_width)[:kept]],
        axis=0,
    )
    query_grad = jnp.concatenate(
        [
            front_query.reshape(CH, local_width)[1:],
            local_query.reshape(row_count, local_width)[:kept],
        ],
        axis=0,
    )
    gate_terms = front_term + local_term
    grad_encoded = key_grad.reshape(span_count, NB, NL, head_count, head_dim)
    normed_grad, context_grad = encoder_backward(grad_encoded, normed, saved)
    gain_grad = normed_grad * gains
    projection = lax.psum(jnp.sum(gain_grad * scaled, axis=(3, 4)), "tensor") / full_width
    neighbour_grad = grad_encoded + inverse * (gain_grad - scaled * projection[..., None, None])
    total_tokens = lax.axis_size("group") * lax.axis_size("dp") * row_count
    summed = lax.psum(gate_terms, ("group", "dp"))
    gate_grad = (1.0 - gate_tanh * gate_tanh) * summed / math.sqrt(total_tokens)
    return (
        cross_output,
        query_grad,
        context_grad.reshape(row_count, local_width).astype(jnp.bfloat16),
        neighbour_grad.reshape(-1, local_width).astype(jnp.bfloat16),
        gate_grad,
    )


def solution(mesh):
    return jax.shard_map(
        shards,
        mesh=mesh,
        in_specs=(
            P(("group", "dp"), "tensor"),
            P(("group", "dp"), "tensor"),
            P(("group", "dp"), "tensor"),
            P("group", None),
            P("tensor"),
            P("tensor"),
            P(("group", "dp"), "tensor"),
        ),
        out_specs=(
            P(("group", "dp"), "tensor"),
            P(("group", "dp"), "tensor"),
            P(("group", "dp"), "tensor"),
            P(("group", "dp"), "tensor"),
            P("tensor"),
        ),
        check_vma=False,
    )
```

profile of v0, /device:TPU:2, one launch (start us, length us, event | category | flops | bytes accessed | tf_op | source)
XLA Modules:
  0.0 361.5 jit_solution(13486729681499176493)
XLA Ops:
  0.6 1.5 fusion.4
  2.2 2.8 convert_bitcast_fusion
  5.0 13.6 %psum.21 = f32[2,2,128]{2,1,0:T(2,128)S(1)} all-reduce(f32[2,2,128]{2,1,0:T(2,128)S(1)} %bitcast.184), channel_id=1, replica_groups=mesh['group'=4,'dp'=32,'tensor'=4] {'tensor'}, use_global_device_ids=true, to_apply=%region_1.0 | all-reduce | flops 512 | bytes 4096 | tf_op jit(solution)/shard_map/psum | solution.py:97
  18.7 2.1 copy.109
  22.5 2.4 fusion.6
  27.2 2.1 collective-permute-start
  30.5 1.2 iota_compare_fusion.1
  32.5 1.9 copy.82
  39.2 1.2 fusion.66
  40.4 5.0 %multiply_reduce_fusion.1 = (f32[8]{0:T(128)}, f32[2,64,8]{1,2,0:T(8,128)}, bf16[2,64,8,128]{3,1,2,0:T(8,128)(2,1)}) fusion(f32[2,64,8,128]{3,2,1,0:T(8,128)} %bitcast.171, f32[8]{0:T(128)} %tanh.3, pred[2]{0:T(512)(128)(4,1)} %get-tuple-element.21, bf16[2,256,8,128]{3,2,1,0:T(8,128)(2,1)S(1)} %bitcast.155, f32[2,8,64]{2,1,0:T(8,128)S(1)} %get-tuple-element.30, ...), kind=kOutput, calls=%fused_computation.63 | convolution fusion | flops 69075192 | bytes 2891842 | tf_op jit(solution)/shard_map/bhrm,bmhd->brhd/dot_general | solution.py:21
  45.4 2.0 fusion.13
  47.4 1.0 fusion.26
  48.4 1.9 fusion.41
  52.5 6.2 %add_bitcast_fusion.1 = f32[2,256,8,128]{1,3,2,0:T(8,128)} fusion(f32[2,8,128,256]{3,2,1,0:T(8,128)} %fusion.41, f32[2,64,8,128]{3,2,1,0:T(8,128)} %bitcast.173, f32[8]{0:T(128)S(1)} %copy-done.14, pred[2]{0:T(512)(128)(4,1)S(1)} %copy-done.16, f32[2,8,64]{2,1,0:T(8,128)S(1)} %get-tuple-element.30, f32[2,8,64,256]{3,2,1,0:T(8,128)} %copy-done.3), kind=kOutput, calls=%fused_computation.18 | convolution fusion | flops 68814080 | bytes 5771298 | tf_op jit(solution)/shard_map/bhrm,brhd->bmhd/dot_general | solution.py:21
  58.6 1.4 fusion.21
  60.9 2.8 multiply_reduce_fusion.3
  63.7 1.6 fusion.24
  65.3 1.3 fusion.45
  66.7 3.4 fusion.17
  70.1 1.3 collective-permute-start.1
  71.4 1.0 fusion.40
  72.4 254.7 %psum.23 = f32[8]{0:T(128)S(1)} all-reduce(f32[8]{0:T(128)S(1)} %add.79), channel_id=1, replica_groups=mesh['group'=4,'dp'=32,'tensor'=4] {'group','dp'}, use_global_device_ids=true, to_apply=%region_15.16 | all-reduce | flops 8 | bytes 64 | tf_op jit(solution)/shard_map/psum | solution.py:155
  327.3 1.3 fusion.27
  330.2 2.3 fusion.28
  332.5 3.0 copy.96
  335.5 1.9 convert_element_type.156
  337.7 2.3 fusion.7
  340.1 1.2 multiply_convert_fusion
  342.8 2.6 multiply_reduce_fusion
  346.3 10.1 %psum.22 = f32[2,2,128]{2,1,0:T(2,128)S(1)} all-reduce(f32[2,2,128]{2,1,0:T(2,128)S(1)} %get-tuple-element.35), channel_id=1, replica_groups=mesh['group'=4,'dp'=32,'tensor'=4] {'tensor'}, use_global_device_ids=true, to_apply=%region_12.13 | all-reduce | flops 512 | bytes 4096 | tf_op jit(solution)/shard_map/psum | solution.py:152
  356.5 3.1 add_convert_fusion
  360.3 1.3 copy.177
  (104 shorter events, 18.2 us)
Async XLA Ops:
  0.6 18.0 %copy-start.10 = (bf16[128,1024]{1,0:T(8,128)(2,1)S(1)}, bf16[128,1024]{1,0:T(8,128)(2,1)}, u32[]{:S(2)}) copy-start(bf16[128,1024]{1,0:T(8,128)(2,1)} %param.10) | copy-start | bytes 786436
  18.7 2.1 copy-start.13
  21.4 1.0 copy-start.1
  21.5 1.0 copy-start.5
  22.4 2.6 copy-start.21
  22.4 2.6 copy-start.23
  24.9 1.0 copy-start.4
  24.9 4.4 %copy-start.15 = (s32[1,64]{1,0:T(1,128)S(1)}, s32[1,64]{1,0:T(1,128)}, u32[]{:S(2)}) copy-start(s32[1,64]{1,0:T(1,128)} %param.12) | copy-start | bytes 772
  24.9 6.8 %copy-start.9 = (bf16[128,1024]{1,0:T(8,128)(2,1)S(1)}, bf16[128,1024]{1,0:T(8,128)(2,1)}, u32[]{:S(2)}) copy-start(bf16[128,1024]{1,0:T(8,128)(2,1)} %param.9) | copy-start | bytes 786436
  25.0 6.9 %copy-start.8 = (bf16[128,1024]{1,0:T(8,128)(2,1)S(1)}, bf16[128,1024]{1,0:T(8,128)(2,1)}, u32[]{:S(2)}) copy-start(bf16[128,1024]{1,0:T(8,128)(2,1)} %param.15) | copy-start | bytes 786436
  26.3 8.2 %copy-start.17 = (f32[8]{0:T(128)S(1)}, f32[8]{0:T(128)}, u32[]{:S(2)}) copy-start(f32[8]{0:T(128)} %param.14) | copy-start | bytes 100
  27.2 31.4 %collective-permute-start = (bf16[256,8,128]{2,0,1:T(8,128)(2,1)}, bf16[256,8,128]{2,0,1:T(8,128)(2,1)}, u32[]{:S(2)}, u32[]{:S(2)}) collective-permute-start(bf16[256,8,128]{2,0,1:T(8,128)(2,1)} %copy.79), channel_id=1, source_target_pairs={{0,4},{4,8},{8,12},{12,16},{16,20},{20,24},{24,28},{28,32},{32,36}... | collective-permute-start | bytes 1572872 | tf_op jit(solution)/shard_map/ppermute | solution.py:17
  38.2 1.0 copy-start.3
  48.4 1.9 slice-start
  48.4 3.4 copy-start.7
  50.3 1.8 copy-start.12
  50.3 2.1 copy-start.20
  50.3 2.1 copy-start.14
  50.3 2.1 copy-start.16
  58.6 2.3 copy-start.11
  65.3 6.0 %copy-start.19 = (f32[8]{0:T(128)S(1)}, f32[8]{0:T(128)}, u32[]{:S(2)}) copy-start(f32[8]{0:T(128)} %get-tuple-element.17) | copy-start | bytes 100
  70.1 260.1 %collective-permute-start.1 = (bf16[256,8,128]{0,2,1:T(8,128)(2,1)}, bf16[256,8,128]{0,2,1:T(8,128)(2,1)S(1)}, u32[]{:S(2)}, u32[]{:S(2)}) collective-permute-start(bf16[256,8,128]{0,2,1:T(8,128)(2,1)} %fusion.17), channel_id=1, source_target_pairs={{4,0},{8,4},{12,8},{16,12},{20,16},{24,20},{28,24},{32,28},{36,32}... | collective-permute-start | bytes 1572872 | tf_op jit(solution)/shard_map/ppermute | solution.py:17
  71.4 258.3 %copy-start.18 = (f32[8]{0:T(128)S(1)}, f32[8]{0:T(128)}, u32[]{:S(2)}) copy-start(f32[8]{0:T(128)} %param.14) | copy-start | bytes 100
  335.5 2.2 copy-start
  335.5 4.6 %copy-start.22 = (f32[2,2,8,128,192]{3,4,2,1,0:T(8,128)S(1)}, f32[2,2,8,128,192]{3,4,2,1,0:T(8,128)}, u32[]{:S(2)}) copy-start(f32[2,2,8,128,192]{3,4,2,1,0:T(8,128)} %copy-done.21) | copy-start | bytes 9437188
  337.7 2.3 copy-start.2
  337.7 2.4 copy-start.6
  337.7 2.4 copy-start.24
where the time goes:
time: 362 us
  blocking collectives  278 us (77%)
  matrix products  36.8 us (10%)
  other arithmetic  22.9 us (6%)
  local copies, waits for them, and re-layouts  18.3 us (5%)
    psum x1, blocking collectives, shards(): summed = lax.psum(gate_terms, ('group', 'dp'))  255 us
    dot_general x18, matrix products, product(): return jnp.einsum(form, left, right, preferred_element_type=jnp.float32)  36.8 us
    psum x1, blocking collectives, shards(): square_sum = lax.psum(jnp.sum(floats * floats, axis=(3, 4)), 'tensor')  13.6 us
    psum x1, blocking collectives, shards(): lax.psum(jnp.sum(gain_grad * scaled, axis=(3, 4)), 'tensor') / full_width  10.1 us
    unnamed x66, local copies, waits for them, and re-layouts  8.57 us
  transfers between devices with their start and end apart: 2, of which 0 were waited for; matrix products, arithmetic and copies ran while one was open for 9% of the time, Pallas kernels for 0%

commit v1 on v0

--- a/solution.py
+++ b/solution.py
@@ -152,7 +152,7 @@
     projection = lax.psum(jnp.sum(gain_grad * scaled, axis=(3, 4)), "tensor") / full_width
     neighbour_grad = grad_encoded + inverse * (gain_grad - scaled * projection[..., None, None])
     total_tokens = lax.axis_size("group") * lax.axis_size("dp") * row_count
-    summed = lax.psum(gate_terms, ("group", "dp"))
+    summed = lax.psum(lax.psum(gate_terms, "dp"), "group")
     gate_grad = (1.0 - gate_tanh * gate_tanh) * summed / math.sqrt(total_tokens)
     return (
         cross_output,

time: 362 us -> 196 us (0.54)
  blocking collectives: 278 us -> 113 us
    psum x1 -> x2, blocking collectives: 255 us -> 89 us  [shards(): summed = lax.psum(lax.psum(gate_terms, 'dp'), 'group')]
  transfers between devices with their start and end apart: 2 -> 2, of which waited for: 0 -> 0; matrix products, arithmetic and copies ran while one was open for 9% -> 16% of each run, Pallas kernels for 0% -> 0%
where the time goes in v1:
time: 196 us
  blocking collectives  113 us (58%)
  matrix products  36.8 us (19%)
  other arithmetic  22.9 us (12%)
  local copies, waits for them, and re-layouts  18.3 us (9%)
  starting transfers between devices  3.38 us (2%)
    psum x2, blocking collectives, shards(): summed = lax.psum(lax.psum(gate_terms, 'dp'), 'group')  89 us
    dot_general x18, matrix products, product(): return jnp.einsum(form, left, right, preferred_element_type=jnp.float32)  36.8 us
    psum x1, blocking collectives, shards(): square_sum = lax.psum(jnp.sum(floats * floats, axis=(3, 4)), 'tensor')  13.6 us
    psum x1, blocking collectives, shards(): lax.psum(jnp.sum(gain_grad * scaled, axis=(3, 4)), 'tensor') / full_width  10.1 us
    unnamed x66, local copies, waits for them, and re-layouts  8.56 us
    unnamed x3, other arithmetic  4.53 us
  transfers between devices with their start and end apart: 2, of which 0 were waited for; matrix products, arithmetic and copies ran while one was open for 16% of the time, Pallas kernels for 0%

profile of v1, /device:TPU:2, one launch (start us, length us, event | category | flops | bytes accessed | tf_op | source)
XLA Modules:
  0.0 195.8 jit_solution(18369152454907057955)
XLA Ops:
  0.6 1.5 fusion.4
  2.2 2.8 %convert_bitcast_fusion = f32[64,8,8,128]{3,1,2,0:T(8,128)} fusion(bf16[512,1024]{1,0:T(8,128)(2,1)} %param.11), kind=kLoop, calls=%fused_computation.8 | loop fusion | flops 524288 | bytes 3145728
  5.0 13.6 %psum.28 = f32[2,2,128]{2,1,0:T(2,128)S(1)} all-reduce(f32[2,2,128]{2,1,0:T(2,128)S(1)} %bitcast.184), channel_id=1, replica_groups=mesh['group'=4,'dp'=32,'tensor'=4] {'tensor'}, use_global_device_ids=true, to_apply=%region_1.0 | all-reduce | flops 512 | bytes 4096 | tf_op jit(solution)/shard_map/psum | solution.py:97
  18.7 2.1 %copy.109 = f32[64,8,8,128]{3,2,1,0:T(8,128)S(1)} copy(f32[64,8,8,128]{3,1,2,0:T(8,128)} %convert_bitcast_fusion) | data formatting | bytes 4194304
  22.5 2.4 %fusion.6 = (bf16[2,2,128,8,128]{4,2,3,1,0:T(8,128)(2,1)S(1)}, f32[2,2,8,128,128]{3,4,2,1,0:T(8,128)}) fusion(f32[2,2,128,8,128]{4,3,2,1,0:T(8,128)S(1)} %bitcast.148, f32[2,2,8,128]{3,2,1,0:T(8,128)S(1)} %get-tuple-element.26, f32[2,2,8,128,192]{3,4,2,1,0:T(8,128)S(1)} %get-tuple-element.27, bf16[2,2,64,8,128]{4,2,3,1,0:T(8,128)(2,1)S(1)} %broadcast_in_dim.103, ...), kind=kOutput, calls=%fused_computation.14 | convolution fusion | flops 207880192 | bytes 9977856 | tf_op jit(solution)/shard_map/cjhqk,cjkhd->cjqhd/dot_general | solution.py:21
  27.2 2.1 %collective-permute-start = (bf16[256,8,128]{2,0,1:T(8,128)(2,1)}, bf16[256,8,128]{2,0,1:T(8,128)(2,1)}, u32[]{:S(2)}, u32[]{:S(2)}) collective-permute-start(bf16[256,8,128]{2,0,1:T(8,128)(2,1)} %copy.79), channel_id=1, source_target_pairs={{0,4},{4,8},{8,12},{12,16},{16,20},{20,24},{24,28},{28,32},{32,36}... | collective-permute-start | bytes 1572872 | tf_op jit(solution)/shard_map/ppermute | solution.py:17
  30.5 1.2 iota_compare_fusion.1
  32.5 1.9 copy.82
  39.2 1.2 fusion.66
  40.4 5.0 %multiply_reduce_fusion.1 = (f32[8]{0:T(128)}, f32[2,64,8]{1,2,0:T(8,128)}, bf16[2,64,8,128]{3,1,2,0:T(8,128)(2,1)}) fusion(f32[2,64,8,128]{3,2,1,0:T(8,128)} %bitcast.171, f32[8]{0:T(128)} %tanh.3, pred[2]{0:T(512)(128)(4,1)} %get-tuple-element.21, bf16[2,256,8,128]{3,2,1,0:T(8,128)(2,1)S(1)} %bitcast.155, f32[2,8,64]{2,1,0:T(8,128)S(1)} %get-tuple-element.30, ...), kind=kOutput, calls=%fused_computation.63 | convolution fusion | flops 69075192 | bytes 2891842 | tf_op jit(solution)/shard_map/bhrm,bmhd->brhd/dot_general | solution.py:21
  45.4 2.0 %fusion.13 = bf16[2,8,64,256]{3,2,1,0:T(8,128)(2,1)S(1)} fusion(bf16[2,256,8,128]{3,2,1,0:T(8,128)(2,1)S(1)} %bitcast.156, f32[2,8,64]{2,1,0:T(8,128)} %bitcast.186, f32[2,8,64,256]{3,2,1,0:T(8,128)} %get-tuple-element.31, f32[2,8,64]{2,1,0:T(8,128)S(1)} %get-tuple-element.30, f32[2,64,8,128]{3,2,1,0:T(8,128)} %bitcast.172, f32[8]{0:T(128)} %tanh.3, ...), kind=kOutput, calls=%fused_computation.30 | convolution fusion | flops 68812800 | bytes 3153954 | tf_op jit(solution)/shard_map/brhd,bmhd->bhrm/dot_general | solution.py:21
  48.4 1.9 fusion.41
  52.5 6.2 %add_bitcast_fusion.1 = f32[2,256,8,128]{1,3,2,0:T(8,128)} fusion(f32[2,8,128,256]{3,2,1,0:T(8,128)} %fusion.41, f32[2,64,8,128]{3,2,1,0:T(8,128)} %bitcast.173, f32[8]{0:T(128)S(1)} %copy-done.14, pred[2]{0:T(512)(128)(4,1)S(1)} %copy-done.16, f32[2,8,64]{2,1,0:T(8,128)S(1)} %get-tuple-element.30, f32[2,8,64,256]{3,2,1,0:T(8,128)} %copy-done.3), kind=kOutput, calls=%fused_computation.18 | convolution fusion | flops 68814080 | bytes 5771298 | tf_op jit(solution)/shard_map/bhrm,brhd->bmhd/dot_general | solution.py:21
  58.6 1.4 fusion.21
  60.9 2.8 %multiply_reduce_fusion.3 = (f32[8]{0:T(128)S(1)}, f32[64,8]{0,1:T(8,128)S(1)}, f32[1,64,8,128]{3,1,2,0:T(8,128)}) fusion(f32[1,64,8,128]{3,2,1,0:T(8,128)S(1)} %bitcast.179, f32[8]{0:T(128)S(1)} %copy-done.14, pred[]{:T(512)S(6)} %and.13, bf16[256,8,128]{2,0,1:T(8,128)(2,1)} %collective-permute-done, f32[8,64]{1,0:T(8,128)S(1)} %get-tuple-element.32, ...), kind=kOutput, calls=%fused_computation.82 | convolution fusion | flops 34406648 | bytes 1577025 | tf_op jit(solution)/shard_map/bhrm,bmhd->brhd/dot_general | solution.py:21
  63.7 1.6 fusion.24
  65.3 1.3 fusion.45
  66.7 3.4 %fusion.17 = bf16[256,8,128]{0,2,1:T(8,128)(2,1)} fusion(f32[8,128,256]{2,1,0:T(8,128)} %fusion.45, f32[8,8,8,128]{3,2,1,0:T(8,128)} %get-tuple-element.24, f32[8]{0:T(128)S(1)} %copy-done.14, pred[]{:T(512)S(6)} %and.13, f32[8,64]{1,0:T(8,128)S(1)} %get-tuple-element.32, f32[8,64,256]{2,1,0:T(8,128)S(1)} %fusion.21), kind=kOutput, calls=%fused_computation.34 | convolution fusion | flops 34669312 | bytes 2361377 | tf_op jit(solution)/shard_map/bhrm,brhd->bmhd/dot_general | solution.py:21
  70.1 1.3 collective-permute-start.1
  71.4 70.2 %psum.30 = f32[8]{0:T(128)S(1)} all-reduce(f32[8]{0:T(128)S(1)} %add.81), channel_id=1, replica_groups=mesh['group'=4,'dp'=32,'tensor'=4] {'dp'}, use_global_device_ids=true, to_apply=%region_15.16 | all-reduce | flops 8 | bytes 64 | tf_op jit(solution)/shard_map/psum | solution.py:155
  141.6 1.1 fusion.40
  142.6 18.8 %psum.31 = f32[8]{0:T(128)S(1)} all-reduce(f32[8]{0:T(128)S(1)} %psum.30), channel_id=1, replica_groups=mesh['group'=4,'dp'=32,'tensor'=4] {'group'}, use_global_device_ids=true, to_apply=%region_16.17 | all-reduce | flops 8 | bytes 64 | tf_op jit(solution)/shard_map/psum | solution.py:155
  161.5 1.3 fusion.27
  164.4 2.3 %fusion.28 = f32[2,256,8,128]{1,3,2,0:T(8,128)} fusion(f32[2,256,8,128]{1,3,2,0:T(8,128)} %add_bitcast_fusion.1, bf16[256,8,128]{0,2,1:T(8,128)(2,1)S(1)} %collective-permute-done.1), kind=kLoop, calls=%fused_computation.54 | loop fusion | flops 524288 | bytes 2621440 | tf_op jit(solution)/shard_map/scatter-add | solution.py:136
  166.8 3.0 %copy.96 = f32[2,256,8,128]{3,2,1,0:T(8,128)} copy(f32[2,256,8,128]{1,3,2,0:T(8,128)} %fusion.28) | data formatting | bytes 4194304 | tf_op jit(solution)/shard_map/scatter-add | solution.py:136
  169.8 1.9 convert_element_type.156
  172.0 2.3 %fusion.7 = f32[2,2,128,8]{2,3,1,0:T(8,128)S(1)} fusion(f32[2,2,8,128,128]{3,4,2,1,0:T(8,128)} %get-tuple-element.29, f32[2,2,128,8,128]{4,3,2,1,0:T(8,128)S(1)} %bitcast.153), kind=kLoop, calls=%fused_computation.15 | loop fusion | flops 1044480 | bytes 4210688 | tf_op jit(solution)/shard_map/reduce_sum | solution.py:43
  174.3 1.2 multiply_convert_fusion
  177.0 2.6 %multiply_reduce_fusion = (f32[2,2,128]{2,1,0:T(2,128)S(1)}, f32[2,2,128,8,128]{4,2,3,1,0:T(8,128)}) fusion(f32[2,2,128,8,128]{4,3,2,1,0:T(8,128)S(1)} %bitcast.149, f32[2,2,128]{2,1,0:T(2,128)S(1)} %add_rsqrt_fusion, f32[8,128]{1,0:T(8,128)S(1)} %bitcast.182, f32[2,2,192,8,128]{4,2,3,1,0:T(8,128)S(1)} %add_bitcast_fusion, ...), kind=kOutput, calls=%fused_computation.17 | convolution fusion | flops 207093248 | bytes 9445376 | tf_op jit(solution)/shard_map/cjhqk,cjkhd->cjqhd/dot_general | solution.py:21
  180.6 10.1 %psum.29 = f32[2,2,128]{2,1,0:T(2,128)S(1)} all-reduce(f32[2,2,128]{2,1,0:T(2,128)S(1)} %get-tuple-element.35), channel_id=1, replica_groups=mesh['group'=4,'dp'=32,'tensor'=4] {'tensor'}, use_global_device_ids=true, to_apply=%region_12.13 | all-reduce | flops 512 | bytes 4096 | tf_op jit(solution)/shard_map/psum | solution.py:152
  190.7 3.1 %add_convert_fusion = bf16[2,2,128,8,128]{4,2,3,1,0:T(8,128)(2,1)S(1)} fusion(f32[2,2,128,8,128]{4,2,3,1,0:T(8,128)} %get-tuple-element.36, f32[2,2,128,8,128]{4,3,2,1,0:T(8,128)} %bitcast.152, f32[2,2,128,8,128]{4,3,2,1,0:T(8,128)S(1)} %bitcast.150, f32[2,2,128]{2,1,0:T(2,128)S(1)} %broadcast_multiply_fusion, f32[2,2,128]{2,1,0:T(2,128)S(1)} %add_rsqrt_fusion), kind=kLoop, calls=%fused_computation.16 | loop fusion | flops 3145728 | bytes 7344128 | tf_op jit(solution)/shard_map/convert_element_type | solution.py:161
  194.5 1.3 copy.177
  (105 shorter events, 19.2 us)
Async XLA Ops:
  0.6 18.0 %copy-start.10 = (bf16[128,1024]{1,0:T(8,128)(2,1)S(1)}, bf16[128,1024]{1,0:T(8,128)(2,1)}, u32[]{:S(2)}) copy-start(bf16[128,1024]{1,0:T(8,128)(2,1)} %param.10) | copy-start | bytes 786436
  18.7 2.1 %copy-start.13 = (f32[1024]{0:T(1024)S(1)}, f32[1024]{0:T(1024)}, u32[]{:S(2)}) copy-start(f32[1024]{0:T(1024)} %param.13) | copy-start | bytes 12292
  21.4 1.0 copy-start.1
  21.5 1.0 copy-start.5
  22.4 2.6 %copy-start.21 = (f32[2,2,8,128,192]{3,4,2,1,0:T(8,128)}, f32[2,2,8,128,192]{3,4,2,1,0:T(8,128)S(1)}, u32[]{:S(2)}) copy-start(f32[2,2,8,128,192]{3,4,2,1,0:T(8,128)S(1)} %get-tuple-element.27) | copy-start | bytes 9437188
  22.4 2.6 %copy-start.23 = (f32[2,2,8,128]{3,2,1,0:T(8,128)}, f32[2,2,8,128]{3,2,1,0:T(8,128)S(1)}, u32[]{:S(2)}) copy-start(f32[2,2,8,128]{3,2,1,0:T(8,128)S(1)} %get-tuple-element.26) | copy-start | bytes 49156
  24.9 1.0 copy-start.4
  24.9 4.4 %copy-start.15 = (s32[1,64]{1,0:T(1,128)S(1)}, s32[1,64]{1,0:T(1,128)}, u32[]{:S(2)}) copy-start(s32[1,64]{1,0:T(1,128)} %param.12) | copy-start | bytes 772
  24.9 6.8 %copy-start.9 = (bf16[128,1024]{1,0:T(8,128)(2,1)S(1)}, bf16[128,1024]{1,0:T(8,128)(2,1)}, u32[]{:S(2)}) copy-start(bf16[128,1024]{1,0:T(8,128)(2,1)} %param.9) | copy-start | bytes 786436
  25.0 6.9 %copy-start.8 = (bf16[128,1024]{1,0:T(8,128)(2,1)S(1)}, bf16[128,1024]{1,0:T(8,128)(2,1)}, u32[]{:S(2)}) copy-start(bf16[128,1024]{1,0:T(8,128)(2,1)} %param.15) | copy-start | bytes 786436
  26.3 8.2 %copy-start.17 = (f32[8]{0:T(128)S(1)}, f32[8]{0:T(128)}, u32[]{:S(2)}) copy-start(f32[8]{0:T(128)} %param.14) | copy-start | bytes 100
  27.2 31.4 %collective-permute-start = (bf16[256,8,128]{2,0,1:T(8,128)(2,1)}, bf16[256,8,128]{2,0,1:T(8,128)(2,1)}, u32[]{:S(2)}, u32[]{:S(2)}) collective-permute-start(bf16[256,8,128]{2,0,1:T(8,128)(2,1)} %copy.79), channel_id=1, source_target_pairs={{0,4},{4,8},{8,12},{12,16},{16,20},{20,24},{24,28},{28,32},{32,36}... | collective-permute-start | bytes 1572872 | tf_op jit(solution)/shard_map/ppermute | solution.py:17
  38.2 1.0 copy-start.3
  48.4 1.9 slice-start
  48.4 3.4 %copy-start.7 = (bf16[2,64,8,128]{3,1,2,0:T(8,128)(2,1)S(1)}, bf16[2,64,8,128]{3,1,2,0:T(8,128)(2,1)}, u32[]{:S(2)}) copy-start(bf16[2,64,8,128]{3,1,2,0:T(8,128)(2,1)} %fusion.26) | copy-start | bytes 786436
  50.3 1.8 copy-start.12
  50.3 2.1 %copy-start.20 = (pred[2]{0:T(512)(128)(4,1)S(1)}, pred[2]{0:T(512)(128)(4,1)}, u32[]{:S(2)}) copy-start(pred[2]{0:T(512)(128)(4,1)} %iota_compare_fusion.1) | copy-start | bytes 10
  50.3 2.1 %copy-start.14 = (f32[8]{0:T(128)S(1)}, f32[8]{0:T(128)}, u32[]{:S(2)}) copy-start(f32[8]{0:T(128)} %tanh.3) | copy-start | bytes 100
  50.3 2.1 %copy-start.16 = (pred[2]{0:T(512)(128)(4,1)S(1)}, pred[2]{0:T(512)(128)(4,1)}, u32[]{:S(2)}) copy-start(pred[2]{0:T(512)(128)(4,1)} %get-tuple-element.21) | copy-start | bytes 10
  58.6 2.3 %copy-start.11 = (f32[8,8,8,128]{3,2,1,0:T(8,128)S(1)}, f32[8,8,8,128]{3,2,1,0:T(8,128)}, u32[]{:S(2)}) copy-start(f32[8,8,8,128]{3,2,1,0:T(8,128)} %copy.115) | copy-start | bytes 786436
  65.3 4.7 %copy-start.19 = (f32[8]{0:T(128)S(1)}, f32[8]{0:T(128)}, u32[]{:S(2)}) copy-start(f32[8]{0:T(128)} %get-tuple-element.17) | copy-start | bytes 100
  70.1 94.3 %collective-permute-start.1 = (bf16[256,8,128]{0,2,1:T(8,128)(2,1)}, bf16[256,8,128]{0,2,1:T(8,128)(2,1)S(1)}, u32[]{:S(2)}, u32[]{:S(2)}) collective-permute-start(bf16[256,8,128]{0,2,1:T(8,128)(2,1)} %fusion.17), channel_id=1, source_target_pairs={{4,0},{8,4},{12,8},{16,12},{20,16},{24,20},{28,24},{32,28},{36,32}... | collective-permute-start | bytes 1572872 | tf_op jit(solution)/shard_map/ppermute | solution.py:17
  141.6 22.3 %copy-start.18 = (f32[8]{0:T(128)S(1)}, f32[8]{0:T(128)}, u32[]{:S(2)}) copy-start(f32[8]{0:T(128)} %param.14) | copy-start | bytes 100
  169.8 2.2 %copy-start = (f32[2,256,8,128]{3,2,1,0:T(8,128)S(1)}, f32[2,256,8,128]{3,2,1,0:T(8,128)}, u32[]{:S(2)}) copy-start(f32[2,256,8,128]{3,2,1,0:T(8,128)} %copy.96) | copy-start | bytes 6291460
  169.8 4.6 %copy-start.22 = (f32[2,2,8,128,192]{3,4,2,1,0:T(8,128)S(1)}, f32[2,2,8,128,192]{3,4,2,1,0:T(8,128)}, u32[]{:S(2)}) copy-start(f32[2,2,8,128,192]{3,4,2,1,0:T(8,128)} %copy-done.21) | copy-start | bytes 9437188
  172.0 2.3 %copy-start.2 = (bf16[2,2,128,8,128]{4,2,3,1,0:T(8,128)(2,1)S(1)}, bf16[2,2,128,8,128]{4,2,3,1,0:T(8,128)(2,1)}, u32[]{:S(2)}) copy-start(bf16[2,2,128,8,128]{4,2,3,1,0:T(8,128)(2,1)} %copy-done.1) | copy-start | bytes 3145732
  172.0 2.4 %copy-start.6 = (bf16[2,2,64,8,128]{4,2,3,1,0:T(8,128)(2,1)S(1)}, bf16[2,2,64,8,128]{4,2,3,1,0:T(8,128)(2,1)}, u32[]{:S(2)}) copy-start(bf16[2,2,64,8,128]{4,2,3,1,0:T(8,128)(2,1)} %copy-done.5) | copy-start | bytes 1572868
  172.0 2.4 %copy-start.24 = (f32[2,2,8,128]{3,2,1,0:T(8,128)S(1)}, f32[2,2,8,128]{3,2,1,0:T(8,128)}, u32[]{:S(2)}) copy-start(f32[2,2,8,128]{3,2,1,0:T(8,128)} %copy-done.23) | copy-start | bytes 49156
